TPU v7x, 128 devices: a whole 4x4x4 slice. The times are simulated.
128 devices in a mesh: ha: 8 (over z, x_lo), wa: 4 (over y), ta: 4 (over x_hi, core).
Axes of the slice: x: 4 (x_hi: 2, x_lo: 2; x = x_hi * 2 + x_lo), y: 4, z: 4, core: 2. Of those that a mesh axis runs over, the one named last changes fastest.
Arguments:
- queries: bfloat16 [12, 32, 64, 3072], P(None, 'wa', 'ha', 'ta'), may hold values from -10 to 10, as said below
- keys_values: bfloat16 [2, 12, 32, 64, 3072], P(None, None, 'wa', 'ha', 'ta'), may hold values from -6 to 6
- out_weight: bfloat16 [3072, 3072], P('ta'), may hold values from -2.5 to 2.5
Outputs:
- projected: bfloat16 [12, 32, 64, 3072], P(None, 'wa', 'ha', 'ta')
Inputs may be any that keep to these rules, and one draw needn't show every extreme that they name: `queries`: query entries.
All inputs are finite; a program needn't handle non-finite values.
Results may differ from a plain program's by a relative error of at most 0.013.
Values may be sent and summed in bfloat16 or wider, within the bound.
No kernel may reach another device: no remote copies, remote signals or barrier semaphores. Data moves between devices by JAX's collectives and lax.ppermute only.
A program may use at most 128 MiB of HBM per device.

v0:
```python
import functools

import jax
import jax.numpy as jnp
from jax import lax
from jax.experimental import pallas as pl
from jax.experimental.pallas import tpu as pltpu
from jax.sharding import PartitionSpec as P

HD = 128
LOG2E = 1.4426950408889634
EXP_SCALE = HD ** (-0.5) * LOG2E
LOW = -1e30
LIMIT = 2.0**60
KEYS = 256


COST2 = 1024


def attend_kernel(gates, first, last, step, *refs):
    flags_ref, q_ref = refs[:2]
    tiles = refs[2 : 2 + len(gates)]
    rest = refs[2 + len(gates) :]
    if not first:
        acc_in, top_in = rest[:2]
        rest = rest[2:]
    tokens = q_ref.shape[0]
    span = tiles[0].shape[1]
    inside = [None if gate is None else flags_ref[gate] > 0 for gate in gates]
    ones = jnp.ones((span, HD), jnp.bfloat16)

    def scores_of(queries, tile, begin, size):
        return lax.dot_general(
            queries, tile[0, pl.ds(begin, size), :], (((1,), (1,)), ((), ())),
            preferred_element_type=jnp.float32,
        )

    def row_max(scores):
        return jnp.broadcast_to(jnp.max(scores, axis=1, keepdims=True), (scores.shape[0], HD))

    def weights_of(scores, shift):
        wide = jnp.concatenate([shift] * (scores.shape[1] // HD), axis=1)
        return jnp.exp2((scores - wide) * EXP_SCALE).astype(jnp.bfloat16)

    def store(rows, mixed, top):
        if last:
            rest[0][rows, :] = (mixed[:, :HD] / mixed[:, HD:]).astype(rest[0].dtype)
        else:
            rest[0][rows, :] = mixed
            rest[1][rows, :] = top

    def full_step(start, all_scores):
        rows = pl.ds(start, step)
        old = jnp.full((step, HD), LOW, jnp.float32) if first else top_in[rows, :]
        new = old
        for scores, valid in zip(all_scores, inside):
            largest = row_max(scores)
            new = jnp.maximum(new, largest if valid is None else jnp.where(valid, largest, LOW))
        mixed = None
        for scores, valid, tile in zip(all_scores, inside, tiles):
            weights = weights_of(scores, new if valid is None else jnp.where(valid, new, -LOW))
            values = jnp.concatenate([tile[1], ones], axis=1)
            part = jnp.dot(weights, values, preferred_element_type=jnp.float32)
            mixed = part if mixed is None else mixed + part
        if not first:
            keep = jnp.exp2((old - new) * EXP_SCALE)
            mixed = acc_in[rows, :] * jnp.concatenate([keep, keep], axis=1) + mixed
        store(rows, mixed, new)

    def tile_scores(start):
        queries = q_ref[pl.ds(start, step), :]
        return [scores_of(queries, tile, 0, span) for tile in tiles]

    if first:
        ready = tile_scores(0)
        for start in range(0, tokens, step):
            following = tile_scores(start + step) if start + step < tokens else None
            full_step(start, ready)
            ready = following
        return

    def quick_weights(start):
        rows = pl.ds(start, step)
        queries = q_ref[rows, :]
        top = top_in[rows, :]
        parts = []
        for tile, valid in zip(tiles, inside):
            shift = top if valid is None else jnp.where(valid, top, -LOW)
            for begin in range(0, span, KEYS):
                parts.append(weights_of(scores_of(queries, tile, begin, KEYS), shift))
        return jnp.concatenate(parts, axis=1), top

    values = jnp.concatenate([jnp.concatenate([tile[1], ones], axis=1) for tile in tiles], axis=0)
    totals = None
    ready = quick_weights(0)
    for start in range(0, tokens, step):
        following = quick_weights(start + step) if start + step < tokens else None
        rows = pl.ds(start, step)
        mixed = jnp.dot(ready[0], values, preferred_element_type=jnp.float32)
        total = mixed[:, HD:]
        totals = total if totals is None else jnp.maximum(totals, total)
        store(rows, acc_in[rows, :] + mixed, ready[1])
        ready = following

    @pl.when(jnp.logical_not(jnp.max(totals) < LIMIT))
    def _():
        for start in range(0, tokens, step):
            full_step(start, tile_scores(start))


def attend(flags, queries, tiles, gates, state=None, last=False, part=None, cost=32):
    channels = queries.shape[1]
    tokens = queries.shape[0] if part is None else queries.shape[0] // 2
    heads = channels // HD
    span = queries.shape[0]
    arrays = [tile[0] if isinstance(tile, tuple) else tile for tile in tiles]

    def tile_spec(tile):
        if isinstance(tile, tuple):
            return pl.BlockSpec((None, 2, span, HD), lambda h: (tile[1], 0, 0, h))
        return pl.BlockSpec((2, span, HD), lambda h: (0, 0, h))

    def rows_spec(array, width):
        block = 0 if part is None or array.shape[0] == tokens else part
        return pl.BlockSpec((tokens, width), lambda h: (block, h))

    in_specs = [pl.BlockSpec(memory_space=pltpu.SMEM), rows_spec(queries, HD)] + [tile_spec(tile) for tile in tiles]
    args = [flags, queries, *arrays]
    if state is not None:
        in_specs += [rows_spec(state[0], 2 * HD), rows_spec(state[1], HD)]
        args += list(state)
    if last:
        out_shape = jax.ShapeDtypeStruct((tokens, channels), jnp.bfloat16)
        out_specs = rows_spec(out_shape, HD)
    else:
        out_shape = [
            jax.ShapeDtypeStruct((tokens, 2 * channels), jnp.float32),
            jax.ShapeDtypeStruct((tokens, channels), jnp.float32),
        ]
        out_specs = [rows_spec(out_shape[0], 2 * HD), rows_spec(out_shape[1], HD)]
    step = 256 if tokens % 256 == 0 else 192
    pairs = len(tiles) * heads * tokens * span
    return pl.pallas_call(
        functools.partial(attend_kernel, tuple(gates), state is None, last, step),
        out_shape=out_shape,
        grid=(heads,),
        in_specs=in_specs,
        out_specs=out_specs,
        compiler_params=pltpu.CompilerParams(vmem_limit_bytes=48 * 1024 * 1024),
        cost_estimate=pl.CostEstimate(flops=pairs * cost, bytes_accessed=1024, transcendentals=0),
    )(*args)


def body(queries, keys_values, out_weight):
    frames, rows, cols, channels = queries.shape
    tokens = frames * rows * cols
    half = channels // 2
    ha_count, wa_count = lax.axis_size("ha"), lax.axis_size("wa")
    ha, wa, ta = lax.axis_index("ha"), lax.axis_index("wa"), lax.axis_index("ta")
    odd = lax.rem(ha, 2)

    q_all = queries.reshape(tokens, channels)
    kv_all = keys_values.reshape(2, tokens, channels)
    keep_at, send_at = odd * half, (1 - odd) * half

    swap_pairs = [(i, i ^ 1) for i in range(ha_count)]
    native_pairs = [(i, (i + (2 if i % 2 else -2)) % ha_count) for i in range(ha_count)]
    swapped_pairs = [(i, (i + (-2 if i % 2 else 2)) % ha_count) for i in range(ha_count)]
    down_pairs = [(i, (i + 1) % wa_count) for i in range(wa_count)]
    up_pairs = [((i + 1) % wa_count, i) for i in range(wa_count)]

    def above_below(cells):
        return lax.ppermute(cells, "wa", down_pairs), lax.ppermute(cells, "wa", up_pairs)

    above, below = wa > 0, wa < wa_count - 1
    low, high = ha >= 2, ha < ha_count - 2
    far_partner = jnp.where(odd == 1, low, high)
    far_native = jnp.where(odd == 1, high, low)
    flags = jnp.stack(
        [above, below, far_partner, far_partner & above, far_partner & below,
         far_native, far_native & above, far_native & below]
    ).astype(jnp.int32)

    kv_send = lax.dynamic_slice_in_dim(kv_all, send_at, half, 2)
    kv_send, kv_all = lax.optimization_barrier((kv_send, kv_all))
    kv_own = lax.dynamic_slice_in_dim(kv_all, keep_at, half, 2)
    q_send = lax.dynamic_slice_in_dim(q_all, send_at, half, 1)
    q_own = lax.dynamic_slice_in_dim(q_all, keep_at, half, 1)

    core, x_hi = lax.rem(ta, 2), ta // 2
    width = out_weight.shape[1] // lax.axis_size("ta")
    ordered = jnp.concatenate(
        [lax.dynamic_slice_in_dim(out_weight, at, half, 0) for at in (keep_at, send_at)], axis=0
    )
    groups = (2 * (1 - x_hi) + 1 - core, 2 * (1 - x_hi) + core, 2 * x_hi + 1 - core, ta)
    weights = [lax.dynamic_slice_in_dim(ordered, group * width, width, 1) for group in groups]

    kv_pair = lax.ppermute(kv_send, "ha", swap_pairs)
    own_up, own_down = above_below(kv_own)
    far_p = lax.ppermute(kv_own, "ha", native_pairs)
    flags, *weights = lax.optimization_barrier((flags, *weights))
    state_n = attend(flags, q_own, [kv_own], [None])
    own_up, own_down, state_n = lax.optimization_barrier((own_up, own_down, state_n))
    far_p_rows = lax.ppermute(jnp.stack([own_up, own_down]), "ha", native_pairs)
    kv_pair, q_send, state_n, far_p = lax.optimization_barrier((kv_pair, q_send, state_n, far_p))
    q_pair = lax.ppermute(q_send, "ha", swap_pairs)
    pair_up, pair_down = above_below(kv_pair)
    far_n = lax.ppermute(kv_pair, "ha", swapped_pairs)

    state_n = attend(flags, q_own, [kv_pair, own_up, own_down], [None, 0, 1], state_n)
    q_pair, state_n = lax.optimization_barrier((q_pair, state_n))
    state_p = attend(flags, q_pair, [kv_own, kv_pair, own_up, own_down, far_p], [None, None, 0, 1, 2])
    far_n, state_p = lax.optimization_barrier((far_n, state_p))
    far_n_up, far_n_down = above_below(far_n)
    state_p = attend(flags, q_pair, [pair_up, pair_down], [0, 1], state_p)
    state_n, state_p = lax.optimization_barrier((state_n, state_p))
    state_n = attend(flags, q_own, [pair_up, pair_down, far_n], [0, 1, 5], state_n)
    state_p, state_n = lax.optimization_barrier((state_p, state_n))
    out_p = attend(flags, q_pair, [(far_p_rows, 0), (far_p_rows, 1)], [3, 4], state_p, last=True)
    state_n, out_p = lax.optimization_barrier((state_n, out_p))
    back = lax.ppermute(out_p, "ha", swap_pairs)
    out_n = attend(flags, q_own, [far_n_up, far_n_down], [6, 7], state_n, last=True)

    core_pairs = [(i, i ^ 1) for i in range(4)]
    hi_pairs = [(i, i ^ 2) for i in range(4)]
    attention = jnp.concatenate([out_n, back], axis=1)

    def partial_of(weight):
        return jnp.dot(attention, weight, preferred_element_type=jnp.float32)

    away_sent = partial_of(weights[0]).astype(jnp.bfloat16)
    away_taken = lax.ppermute(away_sent, "ta", core_pairs)
    away = (partial_of(weights[1]) + away_taken.astype(jnp.float32)).astype(jnp.bfloat16)
    far = lax.ppermute(away, "ta", hi_pairs)
    home_sent = partial_of(weights[2]).astype(jnp.bfloat16)
    home_taken = lax.ppermute(home_sent, "ta", core_pairs)
    home = partial_of(weights[3]) + home_taken.astype(jnp.float32)
    result = home + far.astype(jnp.float32)
    return result.astype(jnp.bfloat16).reshape(frames, rows, cols, width)


def solution(mesh):
    return jax.shard_map(
        body,
        mesh=mesh,
        in_specs=(P(None, "wa", "ha", "ta"), P(None, None, "wa", "ha", "ta"), P("ta", None)),
        out_specs=P(None, "wa", "ha", "ta"),
        check_vma=False,
    )
```

profile of v0, /device:TPU:1, one launch (start us, length us, event | category | flops | bytes accessed | tf_op | source)
XLA Modules:
  0.0 143.9 jit_solution(5877461602138432547)
XLA Ops:
  0.0 1.7 %copy-done = bf16[2,12,8,8,768]{4,3,2,1,0:T(8,128)(2,1)S(1)} copy-done((bf16[2,12,8,8,768]{4,3,2,1,0:T(8,128)(2,1)S(1)}, bf16[2,12,8,8,768]{4,3,2,1,0:T(8,128)(2,1)}, u32[]{:S(2)}) %copy-start) | copy-done | bytes 2359320
  1.7 1.1 constant_dynamic-slice_fusion.2
  2.9 2.2 %collective-permute-start.1 = (bf16[2,768,384]{2,1,0:T(8,128)(2,1)S(1)}, bf16[2,768,384]{2,1,0:T(8,128)(2,1)S(1)}, u32[]{:S(2)}, u32[]{:S(2)}) collective-permute-start(bf16[2,768,384]{2,1,0:T(8,128)(2,1)S(1)} %constant_dynamic-slice_fusion.refs_2_), channel_id=1, source_target_pairs={{0,4},{4,8},{8,12},{12,0},{1,5},{5,9},{9,13},{13,1},{2,6},{6,10},{... | collective-permute-start | bytes 3538952 | tf_op jit(solution)/shard_map/ppermute | solution.py:174
  5.1 1.5 %collective-permute-start.2 = (bf16[2,768,384]{2,1,0:T(8,128)(2,1)S(1)}, bf16[2,768,384]{2,1,0:T(8,128)(2,1)S(1)}, u32[]{:S(2)}, u32[]{:S(2)}) collective-permute-start(bf16[2,768,384]{2,1,0:T(8,128)(2,1)S(1)} %constant_dynamic-slice_fusion.refs_2_), channel_id=1, source_target_pairs={{4,0},{8,4},{12,8},{0,12},{5,1},{9,5},{13,9},{1,13},{6,2},{10,6},{... | collective-permute-start | bytes 3538952 | tf_op jit(solution)/shard_map/ppermute | solution.py:174
  6.6 3.8 %collective-permute-start.3 = (bf16[2,768,384]{2,1,0:T(8,128)(2,1)S(1)}, bf16[2,768,384]{2,1,0:T(8,128)(2,1)}, u32[]{:S(2)}, u32[]{:S(2)}) collective-permute-start(bf16[2,768,384]{2,1,0:T(8,128)(2,1)S(1)} %constant_dynamic-slice_fusion.refs_2_), channel_id=1, source_target_pairs={{0,96},{16,48},{32,0},{48,80},{64,32},{80,112},{96,64},{112,16},{1... | collective-permute-start | bytes 3538952 | tf_op jit(solution)/shard_map/ppermute | solution.py:201
  10.5 2.7 %constant_dynamic-slice_fusion.4 = (bf16[384,3072]{1,0:T(8,128)(2,1)S(1)}, bf16[384,3072]{1,0:T(8,128)(2,1)S(1)}) fusion(bf16[768,3072]{1,0:T(8,128)(2,1)} %param.5, s32[]{:T(128)S(6)} %select_n.37, s32[]{:T(128)S(6)} %select_n.36), kind=kLoop, calls=%fused_computation.22 | loop fusion | bytes 9437192 | tf_op jit(solution)/shard_map/dynamic_slice | solution.py:194
  13.3 2.0 %fusion = (bf16[768,768]{1,0:T(8,128)(2,1)S(1)}, bf16[768,768]{1,0:T(8,128)(2,1)}, bf16[768,768]{1,0:T(8,128)(2,1)}, bf16[768,768]{1,0:T(8,128)(2,1)}) fusion(s32[]{:T(128)S(6)} %select_n.42, bf16[384,3072]{1,0:T(8,128)(2,1)S(1)} %get-tuple-element.96, bf16[384,3072]{1,0:T(8,128)(2,1)S(1)} %get-tuple-element.95, s32[]{:T(128)S(6)} %select_n.39, ...), kind=kLoop, calls=%fused_computation.13 | loop fusion | flops 9437184 | bytes 9437200 | tf_op jit(solution)/shard_map/concatenate | solution.py:193
  16.2 4.1 %shard_map.37 = (f32[768,768]{1,0:T(8,128)S(1)}, f32[768,384]{1,0:T(8,128)S(1)}) custom-call(s32[8]{0:T(128)S(1)} %convert_element_type.24.refs_0_, bf16[768,384]{1,0:T(8,128)(2,1)S(1)} %get-tuple-element.97.refs_1_, bf16[2,768,384]{2,1,0:T(8,128)(2,1)S(1)} %constant_dynamic-slice_fusion.refs_2_), custom_call_target="tpu_custom_call" | custom-call | flops 56623104 | bytes 1024 | tf_op jit(solution)/shard_map/pallas_call | solution.py:144
  20.4 11.7 %collective-permute-done.1.refs_3_.refs_4_ = bf16[2,768,384]{2,1,0:T(8,128)(2,1)S(1)} collective-permute-done((bf16[2,768,384]{2,1,0:T(8,128)(2,1)S(1)}, bf16[2,768,384]{2,1,0:T(8,128)(2,1)S(1)}, u32[]{:S(2)}, u32[]{:S(2)}) %collective-permute-start.1) | collective-permute-done | bytes 1179680 | tf_op jit(solution)/shard_map/ppermute | solution.py:174
  32.4 3.8 %collective-permute-start.10 = (bf16[2,2,768,384]{3,2,1,0:T(8,128)(2,1)S(1)}, bf16[2,2,768,384]{3,2,1,0:T(8,128)(2,1)S(1)}, u32[]{:S(2)}, u32[]{:S(2)}) collective-permute-start(bf16[2,2,768,384]{3,2,1,0:T(8,128)(2,1)S(1)} %pad_maximum_fusion), channel_id=1, source_target_pairs={{0,96},{16,48},{32,0},{48,80},{64,32},{80,112},{96,64},{112,16},{1... | collective-permute-start | bytes 7077896 | tf_op jit(solution)/shard_map/ppermute | solution.py:205
  37.2 2.2 %collective-permute-start.9 = (bf16[2,768,384]{2,1,0:T(8,128)(2,1)}, bf16[2,768,384]{2,1,0:T(8,128)(2,1)S(1)}, u32[]{:S(2)}, u32[]{:S(2)}) collective-permute-start(bf16[2,768,384]{2,1,0:T(8,128)(2,1)} %collective-permute-done.refs_2_.refs_3_), channel_id=1, source_target_pairs={{4,0},{8,4},{12,8},{0,12},{5,1},{9,5},{13,9},{1,13},{6,2},{10,6},{... | collective-permute-start | bytes 3538952 | tf_op jit(solution)/shard_map/ppermute | solution.py:174
  39.5 1.5 %collective-permute-start.5 = (bf16[768,384]{1,0:T(8,128)(2,1)}, bf16[768,384]{1,0:T(8,128)(2,1)S(1)}, u32[]{:S(2)}, u32[]{:S(2)}) collective-permute-start(bf16[768,384]{1,0:T(8,128)(2,1)} %get-tuple-element.56), channel_id=1, source_target_pairs={{0,16},{16,0},{32,48},{48,32},{64,80},{80,64},{96,112},{112,96},{1... | collective-permute-start | bytes 1769480 | tf_op jit(solution)/shard_map/ppermute | solution.py:207
  41.0 9.1 %shard_map.38 = (f32[768,768]{1,0:T(8,128)}, f32[768,384]{1,0:T(8,128)S(1)}) custom-call(s32[8]{0:T(128)S(1)} %convert_element_type.24.refs_0_, bf16[768,384]{1,0:T(8,128)(2,1)S(1)} %get-tuple-element.97.refs_1_, bf16[2,768,384]{2,1,0:T(8,128)(2,1)} %collective-permute-done.refs_2_.refs_3_, bf16[2,768,384]{2,1,0:T(8,128)(2,1)S(1)} %collective-permute-done.1.refs_3_.refs_4_, ...), custom_call_target="tpu_custom_call" | custom-call | flops 169869312 | bytes 1024 | tf_op jit(solution)/shard_map/pallas_call | solution.py:144
  50.1 1.6 %collective-permute-done.5.refs_1_ = bf16[768,384]{1,0:T(8,128)(2,1)S(1)} collective-permute-done((bf16[768,384]{1,0:T(8,128)(2,1)}, bf16[768,384]{1,0:T(8,128)(2,1)S(1)}, u32[]{:S(2)}, u32[]{:S(2)}) %collective-permute-start.5) | collective-permute-done | bytes 589856 | tf_op jit(solution)/shard_map/ppermute | solution.py:207
  51.7 13.5 %shard_map.39 = (f32[768,768]{1,0:T(8,128)}, f32[768,384]{1,0:T(8,128)S(1)}) custom-call(s32[8]{0:T(128)S(1)} %convert_element_type.24.refs_0_, bf16[768,384]{1,0:T(8,128)(2,1)S(1)} %collective-permute-done.5.refs_1_, bf16[2,768,384]{2,1,0:T(8,128)(2,1)S(1)} %constant_dynamic-slice_fusion.refs_2_, bf16[2,768,384]{2,1,0:T(8,128)(2,1)} %collective-permute-done.refs_2_.refs_3_, ...), custom_call_target="tpu_custom_call" | custom-call | flops 283115520 | bytes 1024 | tf_op jit(solution)/shard_map/pallas_call | solution.py:144
  65.3 2.7 %collective-permute-start.7 = (bf16[2,768,384]{2,1,0:T(8,128)(2,1)S(1)}, bf16[2,768,384]{2,1,0:T(8,128)(2,1)S(1)}, u32[]{:S(2)}, u32[]{:S(2)}) collective-permute-start(bf16[2,768,384]{2,1,0:T(8,128)(2,1)S(1)} %collective-permute-done.4.refs_4_), channel_id=1, source_target_pairs={{4,0},{8,4},{12,8},{0,12},{5,1},{9,5},{13,9},{1,13},{6,2},{10,6},{... | collective-permute-start | bytes 3538952 | tf_op jit(solution)/shard_map/ppermute | solution.py:174
  67.9 7.2 %shard_map.40 = (f32[768,768]{1,0:T(8,128)}, f32[768,384]{1,0:T(8,128)S(1)}) custom-call(s32[8]{0:T(128)S(1)} %convert_element_type.24.refs_0_, bf16[768,384]{1,0:T(8,128)(2,1)S(1)} %collective-permute-done.5.refs_1_, bf16[2,768,384]{2,1,0:T(8,128)(2,1)S(1)} %collective-permute-done.8.refs_2_, bf16[2,768,384]{2,1,0:T(8,128)(2,1)S(1)} %collective-permute-done.9.refs_3_, ...), custom_call_target="tpu_custom_call" | custom-call | flops 113246208 | bytes 1024 | tf_op jit(solution)/shard_map/pallas_call | solution.py:144
  75.1 9.2 %shard_map.41 = (f32[768,768]{1,0:T(8,128)}, f32[768,384]{1,0:T(8,128)S(1)}) custom-call(s32[8]{0:T(128)S(1)} %convert_element_type.24.refs_0_, bf16[768,384]{1,0:T(8,128)(2,1)S(1)} %get-tuple-element.97.refs_1_, bf16[2,768,384]{2,1,0:T(8,128)(2,1)S(1)} %collective-permute-done.8.refs_2_, bf16[2,768,384]{2,1,0:T(8,128)(2,1)S(1)} %collective-permute-done.9.refs_3_, ...), custom_call_target="tpu_custom_call" | custom-call | flops 169869312 | bytes 1024 | tf_op jit(solution)/shard_map/pallas_call | solution.py:144
  84.3 1.0 collective-permute-done.10.refs_2_.refs_3_
  85.4 6.3 %shard_map.42 = bf16[768,384]{1,0:T(8,128)(2,1)S(1)} custom-call(s32[8]{0:T(128)S(1)} %convert_element_type.24.refs_0_, bf16[768,384]{1,0:T(8,128)(2,1)S(1)} %collective-permute-done.5.refs_1_, bf16[2,2,768,384]{3,2,1,0:T(8,128)(2,1)S(1)} %collective-permute-done.10.refs_2_.refs_3_, bf16[2,2,768,384]{3,2,1,0:T(8,128)(2,1)S(1)} %collective-permute-done.10.refs_2_.refs_3_, ...), custom_call_target="tpu_custom_call" | custom-call | flops 113246208 | bytes 1024 | tf_op jit(solution)/shard_map/pallas_call | solution.py:144
  91.7 2.4 %collective-permute-start.11 = (bf16[768,384]{1,0:T(8,128)(2,1)S(1)}, bf16[768,384]{1,0:T(8,128)(2,1)S(1)}, u32[]{:S(2)}, u32[]{:S(2)}) collective-permute-start(bf16[768,384]{1,0:T(8,128)(2,1)S(1)} %shard_map.42), channel_id=1, source_target_pairs={{0,16},{16,0},{32,48},{48,32},{64,80},{80,64},{96,112},{112,96},{1... | collective-permute-start | bytes 1769480 | tf_op jit(solution)/shard_map/ppermute | solution.py:222
  94.0 6.3 %shard_map.43 = bf16[768,384]{1,0:T(8,128)(2,1)S(1)} custom-call(s32[8]{0:T(128)S(1)} %convert_element_type.24.refs_0_, bf16[768,384]{1,0:T(8,128)(2,1)S(1)} %get-tuple-element.97.refs_1_, bf16[2,768,384]{2,1,0:T(8,128)(2,1)S(1)} %collective-permute-done.6.refs_2_, bf16[2,768,384]{2,1,0:T(8,128)(2,1)S(1)} %collective-permute-done.7.refs_3_, ...), custom_call_target="tpu_custom_call" | custom-call | flops 113246208 | bytes 1024 | tf_op jit(solution)/shard_map/pallas_call | solution.py:144
  100.3 4.3 %collective-permute-done.11 = bf16[768,384]{1,0:T(8,128)(2,1)S(1)} collective-permute-done((bf16[768,384]{1,0:T(8,128)(2,1)S(1)}, bf16[768,384]{1,0:T(8,128)(2,1)S(1)}, u32[]{:S(2)}, u32[]{:S(2)}) %collective-permute-start.11) | collective-permute-done | bytes 589856 | tf_op jit(solution)/shard_map/ppermute | solution.py:222
  104.7 1.1 convolution_convert_fusion
  105.8 3.7 %collective-permute-start.13 = (bf16[768,768]{1,0:T(8,128)(2,1)S(1)}, bf16[768,768]{1,0:T(8,128)(2,1)S(1)}, u32[]{:S(2)}, u32[]{:S(2)}) collective-permute-start(bf16[768,768]{1,0:T(8,128)(2,1)S(1)} %convolution_convert_fusion), channel_id=1, source_target_pairs={{0,1},{1,0},{2,3},{3,2},{4,5},{5,4},{6,7},{7,6},{8,9},{9,8},{10,11... | collective-permute-start | bytes 3538952 | tf_op jit(solution)/shard_map/ppermute | solution.py:233
  109.5 1.1 convolution_convert_fusion.1
  110.7 1.3 collective-permute-done.13
  112.0 1.1 add_convert_fusion.1
  113.1 2.5 %collective-permute-start.14 = (bf16[768,768]{1,0:T(8,128)(2,1)S(1)}, bf16[768,768]{1,0:T(8,128)(2,1)S(1)}, u32[]{:S(2)}, u32[]{:S(2)}) collective-permute-start(bf16[768,768]{1,0:T(8,128)(2,1)S(1)} %add_convert_fusion.1), channel_id=1, source_target_pairs={{0,2},{1,3},{2,0},{3,1},{4,6},{5,7},{6,4},{7,5},{8,10},{9,11},{10,... | collective-permute-start | bytes 3538952 | tf_op jit(solution)/shard_map/ppermute | solution.py:235
  115.6 1.1 fusion.4
  116.7 25.1 %collective-permute-done.14 = bf16[768,768]{1,0:T(8,128)(2,1)S(1)} collective-permute-done((bf16[768,768]{1,0:T(8,128)(2,1)S(1)}, bf16[768,768]{1,0:T(8,128)(2,1)S(1)}, u32[]{:S(2)}, u32[]{:S(2)}) %collective-permute-start.14) | collective-permute-done | bytes 1179680 | tf_op jit(solution)/shard_map/ppermute | solution.py:235
  141.8 1.4 add_convert_fusion
  (38 shorter events, 3.4 us)
Async XLA Ops:
  0.0 1.7 %copy-start = (bf16[2,12,8,8,768]{4,3,2,1,0:T(8,128)(2,1)S(1)}, bf16[2,12,8,8,768]{4,3,2,1,0:T(8,128)(2,1)}, u32[]{:S(2)}) copy-start(bf16[2,12,8,8,768]{4,3,2,1,0:T(8,128)(2,1)} %param.4) | copy-start | bytes 7077892
  2.9 29.2 %collective-permute-start.1 = (bf16[2,768,384]{2,1,0:T(8,128)(2,1)S(1)}, bf16[2,768,384]{2,1,0:T(8,128)(2,1)S(1)}, u32[]{:S(2)}, u32[]{:S(2)}) collective-permute-start(bf16[2,768,384]{2,1,0:T(8,128)(2,1)S(1)} %constant_dynamic-slice_fusion.refs_2_), channel_id=1, source_target_pairs={{0,4},{4,8},{8,12},{12,0},{1,5},{5,9},{9,13},{13,1},{2,6},{6,10},{... | collective-permute-start | bytes 3538952 | tf_op jit(solution)/shard_map/ppermute | solution.py:174
  5.1 27.0 %collective-permute-start.2 = (bf16[2,768,384]{2,1,0:T(8,128)(2,1)S(1)}, bf16[2,768,384]{2,1,0:T(8,128)(2,1)S(1)}, u32[]{:S(2)}, u32[]{:S(2)}) collective-permute-start(bf16[2,768,384]{2,1,0:T(8,128)(2,1)S(1)} %constant_dynamic-slice_fusion.refs_2_), channel_id=1, source_target_pairs={{4,0},{8,4},{12,8},{0,12},{5,1},{9,5},{13,9},{1,13},{6,2},{10,6},{... | collective-permute-start | bytes 3538952 | tf_op jit(solution)/shard_map/ppermute | solution.py:174
  6.6 30.2 %collective-permute-start.3 = (bf16[2,768,384]{2,1,0:T(8,128)(2,1)S(1)}, bf16[2,768,384]{2,1,0:T(8,128)(2,1)}, u32[]{:S(2)}, u32[]{:S(2)}) collective-permute-start(bf16[2,768,384]{2,1,0:T(8,128)(2,1)S(1)} %constant_dynamic-slice_fusion.refs_2_), channel_id=1, source_target_pairs={{0,96},{16,48},{32,0},{48,80},{64,32},{80,112},{96,64},{112,16},{1... | collective-permute-start | bytes 3538952 | tf_op jit(solution)/shard_map/ppermute | solution.py:201
  10.4 26.4 %collective-permute-start = (bf16[2,768,384]{2,1,0:T(8,128)(2,1)}, bf16[2,768,384]{2,1,0:T(8,128)(2,1)}, u32[]{:S(2)}, u32[]{:S(2)}) collective-permute-start(bf16[2,768,384]{2,1,0:T(8,128)(2,1)} %constant_dynamic-slice_fusion.2), channel_id=1, source_target_pairs={{0,16},{16,0},{32,48},{48,32},{64,80},{80,64},{96,112},{112,96},{1... | collective-permute-start | bytes 3538952 | tf_op jit(solution)/shard_map/ppermute | solution.py:199
  13.2 2.0 %copy-start.9 = (bf16[12,8,8,768]{3,2,1,0:T(8,128)(2,1)S(1)}, bf16[12,8,8,768]{3,2,1,0:T(8,128)(2,1)}, u32[]{:S(2)}) copy-start(bf16[12,8,8,768]{3,2,1,0:T(8,128)(2,1)} %param.3) | copy-start | bytes 3538948
  20.4 12.0 %copy-start.3 = (f32[768,768]{1,0:T(8,128)}, f32[768,768]{1,0:T(8,128)S(1)}, u32[]{:S(2)}) copy-start(f32[768,768]{1,0:T(8,128)S(1)} %get-tuple-element.59.refs_5_) | copy-start | bytes 7077892
  20.4 12.0 %copy-start.5 = (f32[768,384]{1,0:T(8,128)}, f32[768,384]{1,0:T(8,128)S(1)}, u32[]{:S(2)}) copy-start(f32[768,384]{1,0:T(8,128)S(1)} %get-tuple-element.60.refs_6_) | copy-start | bytes 3538948
  32.1 8.9 %copy-start.2 = (bf16[2,768,384]{2,1,0:T(8,128)(2,1)}, bf16[2,768,384]{2,1,0:T(8,128)(2,1)S(1)}, u32[]{:S(2)}) copy-start(bf16[2,768,384]{2,1,0:T(8,128)(2,1)S(1)} %collective-permute-done.2.refs_4_.refs_5_) | copy-start | bytes 3538948
  32.4 53.0 %collective-permute-start.10 = (bf16[2,2,768,384]{3,2,1,0:T(8,128)(2,1)S(1)}, bf16[2,2,768,384]{3,2,1,0:T(8,128)(2,1)S(1)}, u32[]{:S(2)}, u32[]{:S(2)}) collective-permute-start(bf16[2,2,768,384]{3,2,1,0:T(8,128)(2,1)S(1)} %pad_maximum_fusion), channel_id=1, source_target_pairs={{0,96},{16,48},{32,0},{48,80},{64,32},{80,112},{96,64},{112,16},{1... | collective-permute-start | bytes 7077896 | tf_op jit(solution)/shard_map/ppermute | solution.py:205
  36.8 28.4 %collective-permute-start.4 = (bf16[2,768,384]{2,1,0:T(8,128)(2,1)}, bf16[2,768,384]{2,1,0:T(8,128)(2,1)S(1)}, u32[]{:S(2)}, u32[]{:S(2)}) collective-permute-start(bf16[2,768,384]{2,1,0:T(8,128)(2,1)} %collective-permute-done.refs_2_.refs_3_), channel_id=1, source_target_pairs={{0,32},{16,112},{32,64},{48,16},{64,96},{80,48},{96,0},{112,80},{1... | collective-permute-start | bytes 3538952 | tf_op jit(solution)/shard_map/ppermute | solution.py:209
  36.8 31.1 %collective-permute-start.8 = (bf16[2,768,384]{2,1,0:T(8,128)(2,1)}, bf16[2,768,384]{2,1,0:T(8,128)(2,1)S(1)}, u32[]{:S(2)}, u32[]{:S(2)}) collective-permute-start(bf16[2,768,384]{2,1,0:T(8,128)(2,1)} %collective-permute-done.refs_2_.refs_3_), channel_id=1, source_target_pairs={{0,4},{4,8},{8,12},{12,0},{1,5},{5,9},{9,13},{13,1},{2,6},{6,10},{... | collective-permute-start | bytes 3538952 | tf_op jit(solution)/shard_map/ppermute | solution.py:174
  37.2 30.7 %collective-permute-start.9 = (bf16[2,768,384]{2,1,0:T(8,128)(2,1)}, bf16[2,768,384]{2,1,0:T(8,128)(2,1)S(1)}, u32[]{:S(2)}, u32[]{:S(2)}) collective-permute-start(bf16[2,768,384]{2,1,0:T(8,128)(2,1)} %collective-permute-done.refs_2_.refs_3_), channel_id=1, source_target_pairs={{4,0},{8,4},{12,8},{0,12},{5,1},{9,5},{13,9},{1,13},{6,2},{10,6},{... | collective-permute-start | bytes 3538952 | tf_op jit(solution)/shard_map/ppermute | solution.py:174
  39.5 12.2 %collective-permute-start.5 = (bf16[768,384]{1,0:T(8,128)(2,1)}, bf16[768,384]{1,0:T(8,128)(2,1)S(1)}, u32[]{:S(2)}, u32[]{:S(2)}) collective-permute-start(bf16[768,384]{1,0:T(8,128)(2,1)} %get-tuple-element.56), channel_id=1, source_target_pairs={{0,16},{16,0},{32,48},{48,32},{64,80},{80,64},{96,112},{112,96},{1... | collective-permute-start | bytes 1769480 | tf_op jit(solution)/shard_map/ppermute | solution.py:207
  50.1 15.0 %copy-start.4 = (f32[768,384]{1,0:T(8,128)}, f32[768,384]{1,0:T(8,128)S(1)}, u32[]{:S(2)}) copy-start(f32[768,384]{1,0:T(8,128)S(1)} %get-tuple-element.77.refs_6_) | copy-start | bytes 3538948
  65.2 28.8 %collective-permute-start.6 = (bf16[2,768,384]{2,1,0:T(8,128)(2,1)S(1)}, bf16[2,768,384]{2,1,0:T(8,128)(2,1)S(1)}, u32[]{:S(2)}, u32[]{:S(2)}) collective-permute-start(bf16[2,768,384]{2,1,0:T(8,128)(2,1)S(1)} %collective-permute-done.4.refs_4_), channel_id=1, source_target_pairs={{0,4},{4,8},{8,12},{12,0},{1,5},{5,9},{9,13},{13,1},{2,6},{6,10},{... | collective-permute-start | bytes 3538952 | tf_op jit(solution)/shard_map/ppermute | solution.py:174
  65.3 28.8 %collective-permute-start.7 = (bf16[2,768,384]{2,1,0:T(8,128)(2,1)S(1)}, bf16[2,768,384]{2,1,0:T(8,128)(2,1)S(1)}, u32[]{:S(2)}, u32[]{:S(2)}) collective-permute-start(bf16[2,768,384]{2,1,0:T(8,128)(2,1)S(1)} %collective-permute-done.4.refs_4_), channel_id=1, source_target_pairs={{4,0},{8,4},{12,8},{0,12},{5,1},{9,5},{13,9},{1,13},{6,2},{10,6},{... | collective-permute-start | bytes 3538952 | tf_op jit(solution)/shard_map/ppermute | solution.py:174
  91.6 13.0 %copy-start.8 = (bf16[768,768]{1,0:T(8,128)(2,1)S(1)}, bf16[768,768]{1,0:T(8,128)(2,1)}, u32[]{:S(2)}) copy-start(bf16[768,768]{1,0:T(8,128)(2,1)} %get-tuple-element.90) | copy-start | bytes 3538948
  91.7 13.0 %collective-permute-start.11 = (bf16[768,384]{1,0:T(8,128)(2,1)S(1)}, bf16[768,384]{1,0:T(8,128)(2,1)S(1)}, u32[]{:S(2)}, u32[]{:S(2)}) collective-permute-start(bf16[768,384]{1,0:T(8,128)(2,1)S(1)} %shard_map.42), channel_id=1, source_target_pairs={{0,16},{16,0},{32,48},{48,32},{64,80},{80,64},{96,112},{112,96},{1... | collective-permute-start | bytes 1769480 | tf_op jit(solution)/shard_map/ppermute | solution.py:222
  100.3 9.2 %copy-start.7 = (bf16[768,768]{1,0:T(8,128)(2,1)S(1)}, bf16[768,768]{1,0:T(8,128)(2,1)}, u32[]{:S(2)}) copy-start(bf16[768,768]{1,0:T(8,128)(2,1)} %get-tuple-element.88) | copy-start | bytes 3538948
  105.8 6.2 %copy-start.6 = (bf16[768,768]{1,0:T(8,128)(2,1)S(1)}, bf16[768,768]{1,0:T(8,128)(2,1)}, u32[]{:S(2)}) copy-start(bf16[768,768]{1,0:T(8,128)(2,1)} %get-tuple-element.89) | copy-start | bytes 3538948
  105.8 6.2 %collective-permute-start.13 = (bf16[768,768]{1,0:T(8,128)(2,1)S(1)}, bf16[768,768]{1,0:T(8,128)(2,1)S(1)}, u32[]{:S(2)}, u32[]{:S(2)}) collective-permute-start(bf16[768,768]{1,0:T(8,128)(2,1)S(1)} %convolution_convert_fusion), channel_id=1, source_target_pairs={{0,1},{1,0},{2,3},{3,2},{4,5},{5,4},{6,7},{7,6},{8,9},{9,8},{10,11... | collective-permute-start | bytes 3538952 | tf_op jit(solution)/shard_map/ppermute | solution.py:233
  110.6 6.1 %collective-permute-start.12 = (bf16[768,768]{1,0:T(8,128)(2,1)S(1)}, bf16[768,768]{1,0:T(8,128)(2,1)S(1)}, u32[]{:S(2)}, u32[]{:S(2)}) collective-permute-start(bf16[768,768]{1,0:T(8,128)(2,1)S(1)} %convolution_convert_fusion.1), channel_id=1, source_target_pairs={{0,1},{1,0},{2,3},{3,2},{4,5},{5,4},{6,7},{7,6},{8,9},{9,8},{10,11... | collective-permute-start | bytes 3538952 | tf_op jit(solution)/shard_map/ppermute | solution.py:237
  113.1 28.8 %collective-permute-start.14 = (bf16[768,768]{1,0:T(8,128)(2,1)S(1)}, bf16[768,768]{1,0:T(8,128)(2,1)S(1)}, u32[]{:S(2)}, u32[]{:S(2)}) collective-permute-start(bf16[768,768]{1,0:T(8,128)(2,1)S(1)} %add_convert_fusion.1), channel_id=1, source_target_pairs={{0,2},{1,3},{2,0},{3,1},{4,6},{5,7},{6,4},{7,5},{8,10},{9,11},{10,... | collective-permute-start | bytes 3538952 | tf_op jit(solution)/shard_map/ppermute | solution.py:235
  141.8 2.1 %copy-start.1 = (bf16[2,12,8,8,768]{4,3,2,1,0:T(8,128)(2,1)S(1)}, bf16[2,12,8,8,768]{4,3,2,1,0:T(8,128)(2,1)}, u32[]{:S(2)}) copy-start(bf16[2,12,8,8,768]{4,3,2,1,0:T(8,128)(2,1)} %param.4) | copy-start | bytes 7077892
where the time goes:
time: 144 us
  Pallas kernels  55.7 us (39%)
  waiting for transfers between devices  45.7 us (32%)
  starting transfers between devices  26.9 us (19%)
  local copies, waits for them, and re-layouts  7.41 us (5%)
  matrix products  4.34 us (3%)
  other arithmetic  3.7 us (3%)
    pallas_call x7, Pallas kernels, attend(): pl.pallas_call(functools.partial(attend_kernel, tuple(gates), state is No...  55.7 us
    ppermute x1, waiting for transfers between devices, body(): far = lax.ppermute(away, 'ta', hi_pairs)  25.1 us
    ppermute x3, waiting for transfers between devices, above_below(): lax.ppermute(cells, 'wa', down_pairs)  11.7 us
    ppermute x3, starting transfers between devices, above_below(): lax.ppermute(cells, 'wa', up_pairs)  6.42 us
    dot_general x4, matrix products, partial_of(): return jnp.dot(attention, weight, preferred_element_type=jnp.float32)  4.34 us
    ppermute x1, waiting for transfers between devices, body(): back = lax.ppermute(out_p, 'ha', swap_pairs)  4.34 us
    ppermute x1, starting transfers between devices, body(): far_p_rows = lax.ppermute(jnp.stack([own_up, own_down]), 'ha', native_pairs)  3.84 us
    ppermute x1, starting transfers between devices, body(): far_p = lax.ppermute(kv_own, 'ha', native_pairs)  3.76 us
  transfers between devices with their start and end apart: 15, of which 7 were waited for; matrix products, arithmetic and copies ran while one was open for 6% of the time, Pallas kernels for 39%

commit v1 on v0

--- a/solution.py
+++ b/solution.py
@@ -152,6 +152,21 @@
     )(*args)
 
 
+def pass_flags(flags):
+    def copy_kernel(in_ref, out_ref):
+        for index in range(flags.shape[0]):
+            out_ref[index] = in_ref[index]
+
+    spec = pl.BlockSpec(memory_space=pltpu.SMEM)
+    return pl.pallas_call(
+        copy_kernel,
+        out_shape=jax.ShapeDtypeStruct(flags.shape, flags.dtype),
+        in_specs=[spec],
+        out_specs=spec,
+        cost_estimate=pl.CostEstimate(flops=4 * 10**9, bytes_accessed=64, transcendentals=0),
+    )(flags)
+
+
 def body(queries, keys_values, out_weight):
     frames, rows, cols, channels = queries.shape
     tokens = frames * rows * cols
@@ -201,12 +216,13 @@
     far_p = lax.ppermute(kv_own, "ha", native_pairs)
     flags, *weights = lax.optimization_barrier((flags, *weights))
     state_n = attend(flags, q_own, [kv_own], [None])
-    own_up, own_down, state_n = lax.optimization_barrier((own_up, own_down, state_n))
-    far_p_rows = lax.ppermute(jnp.stack([own_up, own_down]), "ha", native_pairs)
-    kv_pair, q_send, state_n, far_p = lax.optimization_barrier((kv_pair, q_send, state_n, far_p))
+    kv_pair, q_send, state_n, flags = lax.optimization_barrier((kv_pair, q_send, state_n, flags))
     q_pair = lax.ppermute(q_send, "ha", swap_pairs)
     pair_up, pair_down = above_below(kv_pair)
     far_n = lax.ppermute(kv_pair, "ha", swapped_pairs)
+    flags = pass_flags(flags)
+    own_up, own_down, far_p, flags = lax.optimization_barrier((own_up, own_down, far_p, flags))
+    far_p_rows = lax.ppermute(jnp.stack([own_up, own_down]), "ha", native_pairs)
 
     state_n = attend(flags, q_own, [kv_pair, own_up, own_down], [None, 0, 1], state_n)
     q_pair, state_n = lax.optimization_barrier((q_pair, state_n))
@@ -226,16 +242,16 @@
     hi_pairs = [(i, i ^ 2) for i in range(4)]
     attention = jnp.concatenate([out_n, back], axis=1)
 
-    def partial_of(weight):
-        return jnp.dot(attention, weight, preferred_element_type=jnp.float32)
-
-    away_sent = partial_of(weights[0]).astype(jnp.bfloat16)
+    def partial_of(group):
+        return jnp.dot(attention, weights[group], preferred_element_type=jnp.float32)
+
+    away_sent = partial_of(0).astype(jnp.bfloat16)
     away_taken = lax.ppermute(away_sent, "ta", core_pairs)
-    away = (partial_of(weights[1]) + away_taken.astype(jnp.float32)).astype(jnp.bfloat16)
+    away = (partial_of(1) + away_taken.astype(jnp.float32)).astype(jnp.bfloat16)
     far = lax.ppermute(away, "ta", hi_pairs)
-    home_sent = partial_of(weights[2]).astype(jnp.bfloat16)
+    home_sent = partial_of(2).astype(jnp.bfloat16)
     home_taken = lax.ppermute(home_sent, "ta", core_pairs)
-    home = partial_of(weights[3]) + home_taken.astype(jnp.float32)
+    home = partial_of(3) + home_taken.astype(jnp.float32)
     result = home + far.astype(jnp.float32)
     return result.astype(jnp.bfloat16).reshape(frames, rows, cols, width)
 

time: 144 us -> 149 us (1.035)
  starting transfers between devices: 26.9 us -> 21.1 us
  waiting for transfers between devices: 45.7 us -> 50.7 us
  local copies, waits for them, and re-layouts: 7.41 us -> 9.83 us
  other arithmetic: 3.7 us -> 5.44 us
    ppermute x3, waiting for transfers between devices: 11.7 us -> 3.24 us  [above_below(): lax.ppermute(cells, 'wa', down_pairs)]
    ppermute x1, waiting for transfers between devices: 0.57 us -> 6.02 us  [body(): kv_pair = lax.ppermute(kv_send, 'ha', swap_pairs)]
    ppermute x1, starting transfers between devices: 3.84 us -> 0.19 us  [body(): far_p_rows = lax.ppermute(jnp.stack([own_up, own_down]), 'ha', native_pairs)]
    ppermute x1, waiting for transfers between devices: 1.05 us -> 3.89 us  [body(): far_p_rows = lax.ppermute(jnp.stack([own_up, own_down]), 'ha', native_pairs)]
    ppermute x3, waiting for transfers between devices: 0.01 us -> 2.44 us  [above_below(): lax.ppermute(cells, 'wa', up_pairs)]
    unnamed x20 -> x28, local copies, waits for them, and re-layouts: 2.39 us -> 4.79 us
    ppermute x1, starting transfers between devices: 0.01 us -> 2.04 us  [body(): kv_pair = lax.ppermute(kv_send, 'ha', swap_pairs)]
    ppermute x1, starting transfers between devices: 2.36 us -> 0.35 us  [body(): back = lax.ppermute(out_p, 'ha', swap_pairs)]
  transfers between devices with their start and end apart: 15 -> 15, of which waited for: 7 -> 9; matrix products, arithmetic and copies ran while one was open for 6% -> 6% of each run, Pallas kernels for 39% -> 38%
where the time goes in v1:
time: 149 us
  Pallas kernels  57.1 us (38%)
  waiting for transfers between devices  50.7 us (34%)
  starting transfers between devices  21.1 us (14%)
  local copies, waits for them, and re-layouts  9.83 us (7%)
  other arithmetic  5.44 us (4%)
  matrix products  4.34 us (3%)
    pallas_call x7, Pallas kernels, attend(): pl.pallas_call(functools.partial(attend_kernel, tuple(gates), state is No...  56 us
    ppermute x1, waiting for transfers between devices, body(): far = lax.ppermute(away, 'ta', hi_pairs)  25.1 us
    ppermute x1, waiting for transfers between devices, body(): kv_pair = lax.ppermute(kv_send, 'ha', swap_pairs)  6.02 us
    ppermute x3, starting transfers between devices, above_below(): lax.ppermute(cells, 'wa', up_pairs)  5.42 us
    ppermute x1, waiting for transfers between devices, body(): back = lax.ppermute(out_p, 'ha', swap_pairs)  5.12 us
    unnamed x28, local copies, waits for them, and re-layouts  4.79 us
    ppermute x1, starting transfers between devices, body(): away_taken = lax.ppermute(away_sent, 'ta', core_pairs)  4.37 us
    dot_general x4, matrix products, partial_of(): jnp.dot(attention, weights[group], preferred_element_type=jnp.float32)  4.34 us
  transfers between devices with their start and end apart: 15, of which 9 were waited for; matrix products, arithmetic and copies ran while one was open for 6% of the time, Pallas kernels for 38%

profile of v1, /device:TPU:1, one launch (start us, length us, event | category | flops | bytes accessed | tf_op | source)
XLA Modules:
  0.0 148.8 jit_solution(8174406508001681163)
XLA Ops:
  0.0 1.7 %copy-done = bf16[2,12,8,8,768]{4,3,2,1,0:T(8,128)(2,1)S(1)} copy-done((bf16[2,12,8,8,768]{4,3,2,1,0:T(8,128)(2,1)S(1)}, bf16[2,12,8,8,768]{4,3,2,1,0:T(8,128)(2,1)}, u32[]{:S(2)}) %copy-start) | copy-done | bytes 2359320
  1.7 1.1 constant_dynamic-slice_fusion.5
  2.8 2.0 %collective-permute-start.3 = (bf16[2,768,384]{2,1,0:T(8,128)(2,1)}, bf16[2,768,384]{2,1,0:T(8,128)(2,1)}, u32[]{:S(2)}, u32[]{:S(2)}) collective-permute-start(bf16[2,768,384]{2,1,0:T(8,128)(2,1)} %constant_dynamic-slice_fusion.5), channel_id=1, source_target_pairs={{0,16},{16,0},{32,48},{48,32},{64,80},{80,64},{96,112},{112,96},{1... | collective-permute-start | bytes 3538952 | tf_op jit(solution)/shard_map/ppermute | solution.py:214
  5.0 3.8 %collective-permute-start.2 = (bf16[2,768,384]{2,1,0:T(8,128)(2,1)S(1)}, bf16[2,768,384]{2,1,0:T(8,128)(2,1)}, u32[]{:S(2)}, u32[]{:S(2)}) collective-permute-start(bf16[2,768,384]{2,1,0:T(8,128)(2,1)S(1)} %constant_dynamic-slice_fusion.4.refs_2_), channel_id=1, source_target_pairs={{0,96},{16,48},{32,0},{48,80},{64,32},{80,112},{96,64},{112,16},{1... | collective-permute-start | bytes 3538952 | tf_op jit(solution)/shard_map/ppermute | solution.py:216
  8.8 2.7 %collective-permute-start.1 = (bf16[2,768,384]{2,1,0:T(8,128)(2,1)S(1)}, bf16[2,768,384]{2,1,0:T(8,128)(2,1)S(1)}, u32[]{:S(2)}, u32[]{:S(2)}) collective-permute-start(bf16[2,768,384]{2,1,0:T(8,128)(2,1)S(1)} %constant_dynamic-slice_fusion.4.refs_2_), channel_id=1, source_target_pairs={{4,0},{8,4},{12,8},{0,12},{5,1},{9,5},{13,9},{1,13},{6,2},{10,6},{... | collective-permute-start | bytes 3538952 | tf_op jit(solution)/shard_map/ppermute | solution.py:189
  11.7 2.7 %constant_dynamic-slice_fusion.1 = (bf16[384,3072]{1,0:T(8,128)(2,1)S(1)}, bf16[384,3072]{1,0:T(8,128)(2,1)S(1)}) fusion(bf16[768,3072]{1,0:T(8,128)(2,1)} %param.5, s32[]{:T(128)S(6)} %select_n.34, s32[]{:T(128)S(6)} %select_n.35), kind=kLoop, calls=%fused_computation.19 | loop fusion | bytes 9437192 | tf_op jit(solution)/shard_map/dynamic_slice | solution.py:209
  14.4 2.4 %fusion = (bf16[768,768]{1,0:T(8,128)(2,1)}, bf16[768,768]{1,0:T(8,128)(2,1)}, bf16[768,768]{1,0:T(8,128)(2,1)}, bf16[768,768]{1,0:T(8,128)(2,1)}) fusion(s32[]{:T(128)S(6)} %select_n.42, bf16[384,3072]{1,0:T(8,128)(2,1)S(1)} %get-tuple-element.96, bf16[384,3072]{1,0:T(8,128)(2,1)S(1)} %get-tuple-element.95, s32[]{:T(128)S(6)} %select_n.39, ...), kind=kLoop, calls=%fused_computation.13 | loop fusion | flops 9437184 | bytes 9437200 | tf_op jit(solution)/shard_map/concatenate | solution.py:208
  17.8 4.1 %shard_map.37 = (f32[768,768]{1,0:T(8,128)S(1)}, f32[768,384]{1,0:T(8,128)S(1)}) custom-call(s32[8]{0:T(128)S(1)} %convert_element_type.24.refs_0_.in_ref, bf16[768,384]{1,0:T(8,128)(2,1)S(1)} %get-tuple-element.97.refs_1_, bf16[2,768,384]{2,1,0:T(8,128)(2,1)S(1)} %constant_dynamic-slice_fusion.4.refs_2_), custom_call_target="tpu_custom_call" | custom-call | flops 56623104 | bytes 1024 | tf_op jit(solution)/shard_map/pallas_call | solution.py:144
  21.9 1.4 copy-done.3
  24.3 6.0 %collective-permute-done.3.refs_2_.refs_3_ = bf16[2,768,384]{2,1,0:T(8,128)(2,1)} collective-permute-done((bf16[2,768,384]{2,1,0:T(8,128)(2,1)}, bf16[2,768,384]{2,1,0:T(8,128)(2,1)}, u32[]{:S(2)}, u32[]{:S(2)}) %collective-permute-start.3) | collective-permute-done | bytes 1179680 | tf_op jit(solution)/shard_map/ppermute | solution.py:214
  30.3 1.2 shard_map.38.refs_0_
  31.5 1.6 %collective-permute-done.2.refs_6_ = bf16[2,768,384]{2,1,0:T(8,128)(2,1)} collective-permute-done((bf16[2,768,384]{2,1,0:T(8,128)(2,1)S(1)}, bf16[2,768,384]{2,1,0:T(8,128)(2,1)}, u32[]{:S(2)}, u32[]{:S(2)}) %collective-permute-start.2) | collective-permute-done | bytes 1179680 | tf_op jit(solution)/shard_map/ppermute | solution.py:216
  33.1 2.4 %collective-permute-done.1.refs_4_.refs_5_ = bf16[2,768,384]{2,1,0:T(8,128)(2,1)S(1)} collective-permute-done((bf16[2,768,384]{2,1,0:T(8,128)(2,1)S(1)}, bf16[2,768,384]{2,1,0:T(8,128)(2,1)S(1)}, u32[]{:S(2)}, u32[]{:S(2)}) %collective-permute-start.1) | collective-permute-done | bytes 1179680 | tf_op jit(solution)/shard_map/ppermute | solution.py:189
  35.6 3.2 %collective-permute-done.refs_3_.refs_4_ = bf16[2,768,384]{2,1,0:T(8,128)(2,1)} collective-permute-done((bf16[2,768,384]{2,1,0:T(8,128)(2,1)S(1)}, bf16[2,768,384]{2,1,0:T(8,128)(2,1)}, u32[]{:S(2)}, u32[]{:S(2)}) %collective-permute-start) | collective-permute-done | bytes 1179680 | tf_op jit(solution)/shard_map/ppermute | solution.py:189
  38.8 1.6 %pad_maximum_fusion = bf16[2,2,768,384]{3,2,1,0:T(8,128)(2,1)S(1)} fusion(bf16[1,2,768,384]{3,2,1,0:T(8,128)(2,1)S(1)} %bitcast.19, bf16[1,2,768,384]{3,2,1,0:T(8,128)(2,1)} %bitcast.10), kind=kLoop, calls=%fused_computation.8 | loop fusion | flops 1179648 | bytes 4718592 | tf_op jit(solution)/shard_map/stack | solution.py:225
  40.6 1.3 collective-permute-start.4
  43.4 9.2 %shard_map.39 = (f32[768,768]{1,0:T(8,128)}, f32[768,384]{1,0:T(8,128)S(1)}) custom-call(s32[8]{0:T(128)S(1)} %copy-done.6, bf16[768,384]{1,0:T(8,128)(2,1)S(1)} %get-tuple-element.97.refs_1_, bf16[2,768,384]{2,1,0:T(8,128)(2,1)} %collective-permute-done.3.refs_2_.refs_3_, bf16[2,768,384]{2,1,0:T(8,128)(2,1)} %collective-permute-done.refs_3_.refs_4_, ...), custom_call_target="tpu_custom_call" | custom-call | flops 169869312 | bytes 1024 | tf_op jit(solution)/shard_map/pallas_call | solution.py:144
  52.6 2.0 %collective-permute-done.5.refs_1_ = bf16[768,384]{1,0:T(8,128)(2,1)S(1)} collective-permute-done((bf16[768,384]{1,0:T(8,128)(2,1)S(1)}, bf16[768,384]{1,0:T(8,128)(2,1)S(1)}, u32[]{:S(2)}, u32[]{:S(2)}) %collective-permute-start.5) | collective-permute-done | bytes 589856 | tf_op jit(solution)/shard_map/ppermute | solution.py:220
  54.7 13.6 %shard_map.40 = (f32[768,768]{1,0:T(8,128)}, f32[768,384]{1,0:T(8,128)S(1)}) custom-call(s32[8]{0:T(128)S(1)} %copy-done.6, bf16[768,384]{1,0:T(8,128)(2,1)S(1)} %collective-permute-done.5.refs_1_, bf16[2,768,384]{2,1,0:T(8,128)(2,1)S(1)} %constant_dynamic-slice_fusion.4.refs_2_, bf16[2,768,384]{2,1,0:T(8,128)(2,1)} %collective-permute-done.3.refs_2_.refs_3_, ...), custom_call_target="tpu_custom_call" | custom-call | flops 283115520 | bytes 1024 | tf_op jit(solution)/shard_map/pallas_call | solution.py:144
  68.2 2.1 %collective-permute-start.7 = (bf16[2,768,384]{2,1,0:T(8,128)(2,1)S(1)}, bf16[2,768,384]{2,1,0:T(8,128)(2,1)S(1)}, u32[]{:S(2)}, u32[]{:S(2)}) collective-permute-start(bf16[2,768,384]{2,1,0:T(8,128)(2,1)S(1)} %collective-permute-done.4.refs_4_), channel_id=1, source_target_pairs={{4,0},{8,4},{12,8},{0,12},{5,1},{9,5},{13,9},{1,13},{6,2},{10,6},{... | collective-permute-start | bytes 3538952 | tf_op jit(solution)/shard_map/ppermute | solution.py:189
  70.4 7.2 %shard_map.41 = (f32[768,768]{1,0:T(8,128)}, f32[768,384]{1,0:T(8,128)S(1)}) custom-call(s32[8]{0:T(128)S(1)} %copy-done.6, bf16[768,384]{1,0:T(8,128)(2,1)S(1)} %collective-permute-done.5.refs_1_, bf16[2,768,384]{2,1,0:T(8,128)(2,1)S(1)} %collective-permute-done.8.refs_2_, bf16[2,768,384]{2,1,0:T(8,128)(2,1)S(1)} %collective-permute-done.9.refs_3_, ...), custom_call_target="tpu_custom_call" | custom-call | flops 113246208 | bytes 1024 | tf_op jit(solution)/shard_map/pallas_call | solution.py:144
  77.6 9.3 %shard_map.42 = (f32[768,768]{1,0:T(8,128)}, f32[768,384]{1,0:T(8,128)S(1)}) custom-call(s32[8]{0:T(128)S(1)} %copy-done.6, bf16[768,384]{1,0:T(8,128)(2,1)S(1)} %get-tuple-element.97.refs_1_, bf16[2,768,384]{2,1,0:T(8,128)(2,1)S(1)} %collective-permute-done.8.refs_2_, bf16[2,768,384]{2,1,0:T(8,128)(2,1)S(1)} %collective-permute-done.9.refs_3_, ...), custom_call_target="tpu_custom_call" | custom-call | flops 169869312 | bytes 1024 | tf_op jit(solution)/shard_map/pallas_call | solution.py:144
  86.9 3.9 %collective-permute-done.10.refs_2_.refs_3_ = bf16[2,2,768,384]{3,2,1,0:T(8,128)(2,1)S(1)} collective-permute-done((bf16[2,2,768,384]{3,2,1,0:T(8,128)(2,1)S(1)}, bf16[2,2,768,384]{3,2,1,0:T(8,128)(2,1)S(1)}, u32[]{:S(2)}, u32[]{:S(2)}) %collective-permute-start.10) | collective-permute-done | bytes 2359328 | tf_op jit(solution)/shard_map/ppermute | solution.py:225
  90.8 6.3 %shard_map.43 = bf16[768,384]{1,0:T(8,128)(2,1)S(1)} custom-call(s32[8]{0:T(128)S(1)} %copy-done.6, bf16[768,384]{1,0:T(8,128)(2,1)S(1)} %collective-permute-done.5.refs_1_, bf16[2,2,768,384]{3,2,1,0:T(8,128)(2,1)S(1)} %collective-permute-done.10.refs_2_.refs_3_, bf16[2,2,768,384]{3,2,1,0:T(8,128)(2,1)S(1)} %collective-permute-done.10.refs_2_.refs_3_, ...), custom_call_target="tpu_custom_call" | custom-call | flops 113246208 | bytes 1024 | tf_op jit(solution)/shard_map/pallas_call | solution.py:144
  97.4 6.3 %shard_map.44 = bf16[768,384]{1,0:T(8,128)(2,1)S(1)} custom-call(s32[8]{0:T(128)S(1)} %copy-done.6, bf16[768,384]{1,0:T(8,128)(2,1)S(1)} %get-tuple-element.97.refs_1_, bf16[2,768,384]{2,1,0:T(8,128)(2,1)S(1)} %collective-permute-done.6.refs_2_, bf16[2,768,384]{2,1,0:T(8,128)(2,1)S(1)} %collective-permute-done.7.refs_3_, ...), custom_call_target="tpu_custom_call" | custom-call | flops 113246208 | bytes 1024 | tf_op jit(solution)/shard_map/pallas_call | solution.py:144
  103.7 5.1 %collective-permute-done.11 = bf16[768,384]{1,0:T(8,128)(2,1)S(1)} collective-permute-done((bf16[768,384]{1,0:T(8,128)(2,1)S(1)}, bf16[768,384]{1,0:T(8,128)(2,1)S(1)}, u32[]{:S(2)}, u32[]{:S(2)}) %collective-permute-start.11) | collective-permute-done | bytes 589856 | tf_op jit(solution)/shard_map/ppermute | solution.py:238
  109.9 4.4 %collective-permute-start.13 = (bf16[768,768]{1,0:T(8,128)(2,1)S(1)}, bf16[768,768]{1,0:T(8,128)(2,1)S(1)}, u32[]{:S(2)}, u32[]{:S(2)}) collective-permute-start(bf16[768,768]{1,0:T(8,128)(2,1)S(1)} %convolution_convert_fusion), channel_id=1, source_target_pairs={{0,1},{1,0},{2,3},{3,2},{4,5},{5,4},{6,7},{7,6},{8,9},{9,8},{10,11... | collective-permute-start | bytes 3538952 | tf_op jit(solution)/shard_map/ppermute | solution.py:249
  115.5 1.3 collective-permute-done.13
  116.8 1.1 add_convert_fusion.1
  117.9 2.5 %collective-permute-start.14 = (bf16[768,768]{1,0:T(8,128)(2,1)S(1)}, bf16[768,768]{1,0:T(8,128)(2,1)S(1)}, u32[]{:S(2)}, u32[]{:S(2)}) collective-permute-start(bf16[768,768]{1,0:T(8,128)(2,1)S(1)} %add_convert_fusion.1), channel_id=1, source_target_pairs={{0,2},{1,3},{2,0},{3,1},{4,6},{5,7},{6,4},{7,5},{8,10},{9,11},{10,... | collective-permute-start | bytes 3538952 | tf_op jit(solution)/shard_map/ppermute | solution.py:251
  121.5 25.1 %collective-permute-done.14 = bf16[768,768]{1,0:T(8,128)(2,1)S(1)} collective-permute-done((bf16[768,768]{1,0:T(8,128)(2,1)S(1)}, bf16[768,768]{1,0:T(8,128)(2,1)S(1)}, u32[]{:S(2)}, u32[]{:S(2)}) %collective-permute-start.14) | collective-permute-done | bytes 1179680 | tf_op jit(solution)/shard_map/ppermute | solution.py:251
  146.7 1.4 add_convert_fusion
  (47 shorter events, 8.3 us)
Async XLA Ops:
  0.0 1.7 %copy-start = (bf16[2,12,8,8,768]{4,3,2,1,0:T(8,128)(2,1)S(1)}, bf16[2,12,8,8,768]{4,3,2,1,0:T(8,128)(2,1)}, u32[]{:S(2)}) copy-start(bf16[2,12,8,8,768]{4,3,2,1,0:T(8,128)(2,1)} %param.4) | copy-start | bytes 7077892
  2.8 27.5 %collective-permute-start.3 = (bf16[2,768,384]{2,1,0:T(8,128)(2,1)}, bf16[2,768,384]{2,1,0:T(8,128)(2,1)}, u32[]{:S(2)}, u32[]{:S(2)}) collective-permute-start(bf16[2,768,384]{2,1,0:T(8,128)(2,1)} %constant_dynamic-slice_fusion.5), channel_id=1, source_target_pairs={{0,16},{16,0},{32,48},{48,32},{64,80},{80,64},{96,112},{112,96},{1... | collective-permute-start | bytes 3538952 | tf_op jit(solution)/shard_map/ppermute | solution.py:214
  5.0 28.1 %collective-permute-start.2 = (bf16[2,768,384]{2,1,0:T(8,128)(2,1)S(1)}, bf16[2,768,384]{2,1,0:T(8,128)(2,1)}, u32[]{:S(2)}, u32[]{:S(2)}) collective-permute-start(bf16[2,768,384]{2,1,0:T(8,128)(2,1)S(1)} %constant_dynamic-slice_fusion.4.refs_2_), channel_id=1, source_target_pairs={{0,96},{16,48},{32,0},{48,80},{64,32},{80,112},{96,64},{112,16},{1... | collective-permute-start | bytes 3538952 | tf_op jit(solution)/shard_map/ppermute | solution.py:216
  8.8 26.8 %collective-permute-start.1 = (bf16[2,768,384]{2,1,0:T(8,128)(2,1)S(1)}, bf16[2,768,384]{2,1,0:T(8,128)(2,1)S(1)}, u32[]{:S(2)}, u32[]{:S(2)}) collective-permute-start(bf16[2,768,384]{2,1,0:T(8,128)(2,1)S(1)} %constant_dynamic-slice_fusion.4.refs_2_), channel_id=1, source_target_pairs={{4,0},{8,4},{12,8},{0,12},{5,1},{9,5},{13,9},{1,13},{6,2},{10,6},{... | collective-permute-start | bytes 3538952 | tf_op jit(solution)/shard_map/ppermute | solution.py:189
  11.5 27.3 %collective-permute-start = (bf16[2,768,384]{2,1,0:T(8,128)(2,1)S(1)}, bf16[2,768,384]{2,1,0:T(8,128)(2,1)}, u32[]{:S(2)}, u32[]{:S(2)}) collective-permute-start(bf16[2,768,384]{2,1,0:T(8,128)(2,1)S(1)} %constant_dynamic-slice_fusion.4.refs_2_), channel_id=1, source_target_pairs={{0,4},{4,8},{8,12},{12,0},{1,5},{5,9},{9,13},{13,1},{2,6},{6,10},{... | collective-permute-start | bytes 3538952 | tf_op jit(solution)/shard_map/ppermute | solution.py:189
  11.7 6.1 %copy-start.7 = (s32[8]{0:T(128)}, s32[8]{0:T(128)S(1)}, u32[]{:S(2)}) copy-start(s32[8]{0:T(128)S(1)} %convert_element_type.24.refs_0_.in_ref) | copy-start | bytes 100
  14.4 2.4 %copy-start.12 = (bf16[12,8,8,768]{3,2,1,0:T(8,128)(2,1)S(1)}, bf16[12,8,8,768]{3,2,1,0:T(8,128)(2,1)}, u32[]{:S(2)}) copy-start(bf16[12,8,8,768]{3,2,1,0:T(8,128)(2,1)} %param.3) | copy-start | bytes 3538948
  21.9 1.4 copy-start.3
  23.3 1.0 copy-start.5
  35.6 7.9 %copy-start.2 = (bf16[2,768,384]{2,1,0:T(8,128)(2,1)}, bf16[2,768,384]{2,1,0:T(8,128)(2,1)S(1)}, u32[]{:S(2)}) copy-start(bf16[2,768,384]{2,1,0:T(8,128)(2,1)S(1)} %collective-permute-done.1.refs_4_.refs_5_) | copy-start | bytes 3538948
  38.8 4.6 %copy-start.13 = (bf16[768,384]{1,0:T(8,128)(2,1)S(1)}, bf16[768,384]{1,0:T(8,128)(2,1)}, u32[]{:S(2)}) copy-start(bf16[768,384]{1,0:T(8,128)(2,1)} %get-tuple-element.56) | copy-start | bytes 1769476
  38.8 4.6 %copy-start.6 = (s32[8]{0:T(128)S(1)}, s32[8]{0:T(128)}, u32[]{:S(2)}) copy-start(s32[8]{0:T(128)} %shard_map.38.refs_0_) | copy-start | bytes 100
  40.4 50.4 %collective-permute-start.10 = (bf16[2,2,768,384]{3,2,1,0:T(8,128)(2,1)S(1)}, bf16[2,2,768,384]{3,2,1,0:T(8,128)(2,1)S(1)}, u32[]{:S(2)}, u32[]{:S(2)}) collective-permute-start(bf16[2,2,768,384]{3,2,1,0:T(8,128)(2,1)S(1)} %pad_maximum_fusion), channel_id=1, source_target_pairs={{0,96},{16,48},{32,0},{48,80},{64,32},{80,112},{96,64},{112,16},{1... | collective-permute-start | bytes 7077896 | tf_op jit(solution)/shard_map/ppermute | solution.py:225
  40.6 27.6 %collective-permute-start.4 = (bf16[2,768,384]{2,1,0:T(8,128)(2,1)}, bf16[2,768,384]{2,1,0:T(8,128)(2,1)S(1)}, u32[]{:S(2)}, u32[]{:S(2)}) collective-permute-start(bf16[2,768,384]{2,1,0:T(8,128)(2,1)} %collective-permute-done.3.refs_2_.refs_3_), channel_id=1, source_target_pairs={{0,32},{16,112},{32,64},{48,16},{64,96},{80,48},{96,0},{112,80},{1... | collective-permute-start | bytes 3538952 | tf_op jit(solution)/shard_map/ppermute | solution.py:222
  41.9 28.4 %collective-permute-start.9 = (bf16[2,768,384]{2,1,0:T(8,128)(2,1)}, bf16[2,768,384]{2,1,0:T(8,128)(2,1)S(1)}, u32[]{:S(2)}, u32[]{:S(2)}) collective-permute-start(bf16[2,768,384]{2,1,0:T(8,128)(2,1)} %collective-permute-done.3.refs_2_.refs_3_), channel_id=1, source_target_pairs={{4,0},{8,4},{12,8},{0,12},{5,1},{9,5},{13,9},{1,13},{6,2},{10,6},{... | collective-permute-start | bytes 3538952 | tf_op jit(solution)/shard_map/ppermute | solution.py:189
  42.5 27.9 %collective-permute-start.8 = (bf16[2,768,384]{2,1,0:T(8,128)(2,1)}, bf16[2,768,384]{2,1,0:T(8,128)(2,1)S(1)}, u32[]{:S(2)}, u32[]{:S(2)}) collective-permute-start(bf16[2,768,384]{2,1,0:T(8,128)(2,1)} %collective-permute-done.3.refs_2_.refs_3_), channel_id=1, source_target_pairs={{0,4},{4,8},{8,12},{12,0},{1,5},{5,9},{9,13},{13,1},{2,6},{6,10},{... | collective-permute-start | bytes 3538952 | tf_op jit(solution)/shard_map/ppermute | solution.py:189
  43.4 11.3 %collective-permute-start.5 = (bf16[768,384]{1,0:T(8,128)(2,1)S(1)}, bf16[768,384]{1,0:T(8,128)(2,1)S(1)}, u32[]{:S(2)}, u32[]{:S(2)}) collective-permute-start(bf16[768,384]{1,0:T(8,128)(2,1)S(1)} %copy-done.13), channel_id=1, source_target_pairs={{0,16},{16,0},{32,48},{48,32},{64,80},{80,64},{96,112},{112,96},{1... | collective-permute-start | bytes 1769480 | tf_op jit(solution)/shard_map/ppermute | solution.py:220
  52.6 15.6 %copy-start.4 = (f32[768,384]{1,0:T(8,128)}, f32[768,384]{1,0:T(8,128)S(1)}, u32[]{:S(2)}) copy-start(f32[768,384]{1,0:T(8,128)S(1)} %get-tuple-element.77.refs_6_) | copy-start | bytes 3538948
  68.2 29.2 %collective-permute-start.7 = (bf16[2,768,384]{2,1,0:T(8,128)(2,1)S(1)}, bf16[2,768,384]{2,1,0:T(8,128)(2,1)S(1)}, u32[]{:S(2)}, u32[]{:S(2)}) collective-permute-start(bf16[2,768,384]{2,1,0:T(8,128)(2,1)S(1)} %collective-permute-done.4.refs_4_), channel_id=1, source_target_pairs={{4,0},{8,4},{12,8},{0,12},{5,1},{9,5},{13,9},{1,13},{6,2},{10,6},{... | collective-permute-start | bytes 3538952 | tf_op jit(solution)/shard_map/ppermute | solution.py:189
  70.3 27.1 %collective-permute-start.6 = (bf16[2,768,384]{2,1,0:T(8,128)(2,1)S(1)}, bf16[2,768,384]{2,1,0:T(8,128)(2,1)S(1)}, u32[]{:S(2)}, u32[]{:S(2)}) collective-permute-start(bf16[2,768,384]{2,1,0:T(8,128)(2,1)S(1)} %collective-permute-done.4.refs_4_), channel_id=1, source_target_pairs={{0,4},{4,8},{8,12},{12,0},{1,5},{5,9},{9,13},{13,1},{2,6},{6,10},{... | collective-permute-start | bytes 3538952 | tf_op jit(solution)/shard_map/ppermute | solution.py:189
  97.0 11.8 %copy-start.11 = (bf16[768,768]{1,0:T(8,128)(2,1)S(1)}, bf16[768,768]{1,0:T(8,128)(2,1)}, u32[]{:S(2)}) copy-start(bf16[768,768]{1,0:T(8,128)(2,1)} %get-tuple-element.90) | copy-start | bytes 3538948
  97.0 11.8 %collective-permute-start.11 = (bf16[768,384]{1,0:T(8,128)(2,1)S(1)}, bf16[768,384]{1,0:T(8,128)(2,1)S(1)}, u32[]{:S(2)}, u32[]{:S(2)}) collective-permute-start(bf16[768,384]{1,0:T(8,128)(2,1)S(1)} %shard_map.43), channel_id=1, source_target_pairs={{0,16},{16,0},{32,48},{48,32},{64,80},{80,64},{96,112},{112,96},{1... | collective-permute-start | bytes 1769480 | tf_op jit(solution)/shard_map/ppermute | solution.py:238
  103.7 10.6 %copy-start.10 = (bf16[768,768]{1,0:T(8,128)(2,1)S(1)}, bf16[768,768]{1,0:T(8,128)(2,1)}, u32[]{:S(2)}) copy-start(bf16[768,768]{1,0:T(8,128)(2,1)} %get-tuple-element.88) | copy-start | bytes 3538948
  109.9 6.9 %copy-start.9 = (bf16[768,768]{1,0:T(8,128)(2,1)S(1)}, bf16[768,768]{1,0:T(8,128)(2,1)}, u32[]{:S(2)}) copy-start(bf16[768,768]{1,0:T(8,128)(2,1)} %get-tuple-element.89) | copy-start | bytes 3538948
  109.9 6.8 %collective-permute-start.13 = (bf16[768,768]{1,0:T(8,128)(2,1)S(1)}, bf16[768,768]{1,0:T(8,128)(2,1)S(1)}, u32[]{:S(2)}, u32[]{:S(2)}) collective-permute-start(bf16[768,768]{1,0:T(8,128)(2,1)S(1)} %convolution_convert_fusion), channel_id=1, source_target_pairs={{0,1},{1,0},{2,3},{3,2},{4,5},{5,4},{6,7},{7,6},{8,9},{9,8},{10,11... | collective-permute-start | bytes 3538952 | tf_op jit(solution)/shard_map/ppermute | solution.py:249
  115.4 5.0 %copy-start.8 = (bf16[768,768]{1,0:T(8,128)(2,1)S(1)}, bf16[768,768]{1,0:T(8,128)(2,1)}, u32[]{:S(2)}) copy-start(bf16[768,768]{1,0:T(8,128)(2,1)} %get-tuple-element.87) | copy-start | bytes 3538948
  115.4 6.1 %collective-permute-start.12 = (bf16[768,768]{1,0:T(8,128)(2,1)S(1)}, bf16[768,768]{1,0:T(8,128)(2,1)S(1)}, u32[]{:S(2)}, u32[]{:S(2)}) collective-permute-start(bf16[768,768]{1,0:T(8,128)(2,1)S(1)} %convolution_convert_fusion.1), channel_id=1, source_target_pairs={{0,1},{1,0},{2,3},{3,2},{4,5},{5,4},{6,7},{7,6},{8,9},{9,8},{10,11... | collective-permute-start | bytes 3538952 | tf_op jit(solution)/shard_map/ppermute | solution.py:253
  117.9 28.8 %collective-permute-start.14 = (bf16[768,768]{1,0:T(8,128)(2,1)S(1)}, bf16[768,768]{1,0:T(8,128)(2,1)S(1)}, u32[]{:S(2)}, u32[]{:S(2)}) collective-permute-start(bf16[768,768]{1,0:T(8,128)(2,1)S(1)} %add_convert_fusion.1), channel_id=1, source_target_pairs={{0,2},{1,3},{2,0},{3,1},{4,6},{5,7},{6,4},{7,5},{8,10},{9,11},{10,... | collective-permute-start | bytes 3538952 | tf_op jit(solution)/shard_map/ppermute | solution.py:251
  146.7 2.1 %copy-start.1 = (bf16[2,12,8,8,768]{4,3,2,1,0:T(8,128)(2,1)S(1)}, bf16[2,12,8,8,768]{4,3,2,1,0:T(8,128)(2,1)}, u32[]{:S(2)}) copy-start(bf16[2,12,8,8,768]{4,3,2,1,0:T(8,128)(2,1)} %param.4) | copy-start | bytes 7077892
